TPU v7x, 32 devices: a whole 2x2x4 slice. The times are simulated.
32 devices in a mesh: grp: 2 (over y), bl: 4 (over z), ch: 2 (over x), pol: 2 (over core).
Axes of the slice: x: 2, y: 2, z: 4, core: 2. Of those that a mesh axis runs over, the one named last changes fastest.
Arguments:
- visibility: float32 [4, 2, 2, 384, 1024], P('pol', None, None, 'ch', ('grp', 'bl')), parts along dimension 4, may hold values from -6 to 6
- uv_coords: float32 [2, 2, 1024], P(None, None, ('grp', 'bl')), parts along dimension 2, may hold values from -3072 to 3072
- source_lm: float32 [2, 64], replicated, may hold values from -0.1 to 0.1
- source_flux: float32 [4, 64], P('pol'), may hold values from -1 to 1
- avg_factor: int32 [1024], P(('grp', 'bl')), parts along dimension 0, may hold values from 1 to 2, as said below
- station_pairs: int32 [2, 1024], P(None, ('grp', 'bl')), parts along dimension 1, may hold values from 0 to 511, as said below
- slot_owner: int32 [2], replicated, may hold values from 0 to 1, each once
Outputs:
- residual: float32 [4, 2, 2, 384, 1024], P('pol', None, 'ch', None, ('grp', 'bl')), parts along dimension 4
- gains: float32 [3, 2, 2, 1024], P(None, None, 'ch', 'grp'), parts along dimension 3
There are 2 independent parts, one for each index of `grp`. A program takes and returns all parts, laid end to end along the dimension named above; an argument that names none is the same for every part. Nothing has to cross between parts.
Inputs may be any that keep to these rules, and one draw needn't show every extreme that they name: `avg_factor`: each factor is a power of two. `station_pairs`: the two stations of a baseline differ; the first stations of the baselines in aligned blocks of 128 rows lie in the matching block of 128 stations. `slot_owner`: each position occurs once.
All inputs are finite; a program needn't handle non-finite values.
Results may differ from a plain program's by a relative error of at most 0.0003.
Values sent between devices are 32-bit elements; how exact they have to be, the bound alone decides.
A program may use at most 64 MiB of HBM per device.

v0:
```python
import jax
import jax.numpy as jnp
from jax import lax
from jax.sharding import PartitionSpec as P

STATIONS = 512
SRC_BLOCK = 16
ITERS = 3


damping = 1.0
two_pi = 6.283185307179586
highest = lax.Precision.HIGHEST


def averaging_weights(avg_factor, slot_count):
    slot_index = jnp.arange(slot_count, dtype=jnp.int32)
    factor = avg_factor[None, None, :]
    same_group = slot_index[:, None, None] // factor == slot_index[None, :, None] // factor
    return same_group.astype(jnp.float32) / factor.astype(jnp.float32)


def owner_slots(slot_owner):
    slot_index = jnp.arange(slot_owner.shape[0], dtype=jnp.int32)
    match_table = slot_owner[:, None] == slot_index[None, :]
    return jnp.sum(jnp.where(match_table, slot_index[:, None], 0), axis=0)


def predict_slot(uv_slot, source_lm, source_flux, frequency, block_size):
    geometry = (
        source_lm[0][:, None] * uv_slot[0][None, :] + source_lm[1][:, None] * uv_slot[1][None, :]
    )
    start_value = jnp.zeros(
        (source_flux.shape[0], 2, frequency.shape[0], uv_slot.shape[1]), jnp.float32
    )

    def add_block(block_number, running_total):
        first_source = (block_number * block_size).astype(jnp.int32)
        geo_block = lax.dynamic_slice_in_dim(geometry, first_source, block_size, 0)
        flux_block = lax.dynamic_slice_in_dim(source_flux, first_source, block_size, 1)
        phase_angle = -two_pi * frequency[None, :, None] * geo_block[:, None, :]
        real_part = jnp.einsum("ks,scb->kcb", flux_block, jnp.cos(phase_angle), precision=highest)
        imag_part = jnp.einsum("ks,scb->kcb", flux_block, jnp.sin(phase_angle), precision=highest)
        return running_total + jnp.stack([real_part, imag_part], axis=1)

    return lax.fori_loop(0, geometry.shape[0] // block_size, add_block, start_value)


def averaged_rows(row_weights, slot_values, row_shape):

    def add_slot(slot_number, running_total):
        weight = lax.dynamic_index_in_dim(row_weights, slot_number, 1, keepdims=False)
        return running_total + weight[None, None, :, None, :] * slot_values(slot_number)[:, :, None]

    return lax.fori_loop(0, row_weights.shape[1], add_slot, jnp.zeros(row_shape, jnp.float32))


def model_residual(
    data_rows, model_rows, gains, first_station, second_station, first_pol, frequency
):
    own_pol = lax.dynamic_index_in_dim(gains, first_pol, 1, keepdims=False)
    first_gain = jnp.take(own_pol, first_station, axis=2)[:, None, :, None, :]
    second_gain = jnp.take(gains, second_station, axis=3)[:, :, :, None, :]
    angular = two_pi * frequency[None, None, :, None]
    phase_angle = angular * (first_gain[2] - second_gain[2])
    cos_phase = jnp.cos(phase_angle)
    sin_phase = jnp.sin(phase_angle)
    model_real = model_rows[:, 0]
    model_imag = model_rows[:, 1]
    turned_real = cos_phase * model_real - sin_phase * model_imag
    turned_imag = sin_phase * model_real + cos_phase * model_imag
    conj_real = second_gain[0] * turned_real + second_gain[1] * turned_imag
    conj_imag = second_gain[0] * turned_imag - second_gain[1] * turned_real
    lead_real = first_gain[0] * turned_real - first_gain[1] * turned_imag
    lead_imag = first_gain[0] * turned_imag + first_gain[1] * turned_real
    pred_real = first_gain[0] * conj_real - first_gain[1] * conj_imag
    pred_imag = first_gain[0] * conj_imag + first_gain[1] * conj_real
    resid_real = data_rows[:, 0] - pred_real
    resid_imag = data_rows[:, 1] - pred_imag
    return (
        resid_real,
        resid_imag,
        conj_real,
        conj_imag,
        lead_real,
        lead_imag,
        pred_real,
        pred_imag,
        angular,
    )


def normal_terms(pieces, first_hot, second_hot, first_pol):
    (
        resid_real,
        resid_imag,
        conj_real,
        conj_imag,
        lead_real,
        lead_imag,
        pred_real,
        pred_imag,
        angular,
    ) = pieces
    conj_power = conj_real * conj_real + conj_imag * conj_imag
    lead_power = lead_real * lead_real + lead_imag * lead_imag
    squared = angular * angular
    pred_cross = pred_real * resid_imag - pred_imag * resid_real
    first_terms = jnp.stack(
        [
            jnp.sum(conj_power, axis=(0, 2)),
            jnp.sum(angular * conj_power, axis=(0, 2)),
            jnp.sum(squared * conj_power, axis=(0, 2)),
            jnp.sum(conj_real * resid_real + conj_imag * resid_imag, axis=(0, 2)),
            jnp.sum(conj_real * resid_imag - conj_imag * resid_real, axis=(0, 2)),
            jnp.sum(angular * pred_cross, axis=(0, 2)),
        ]
    )
    second_terms = jnp.stack(
        [
            jnp.sum(lead_power, axis=2),
            jnp.sum(angular * lead_power, axis=2),
            jnp.sum(squared * lead_power, axis=2),
            jnp.sum(lead_real * resid_real + lead_imag * resid_imag, axis=2),
            -jnp.sum(lead_real * resid_imag - lead_imag * resid_real, axis=2),
            -jnp.sum(angular * pred_cross, axis=2),
        ]
    )
    first_sums = jnp.einsum("xnb,bs->xns", first_terms, first_hot, precision=highest)
    second_sums = jnp.einsum("xqnb,bs->xqns", second_terms, second_hot, precision=highest)
    select = (jnp.arange(2) == first_pol).astype(jnp.float32)
    return second_sums + first_sums[:, None] * select[None, :, None, None]


def gain_update(gains, normals):
    real_gain = gains[0]
    imag_gain = gains[1]
    delay = gains[2]
    diagonal = (1.0 + damping) * normals[0] + 1.0
    cross_real = -imag_gain * normals[1]
    cross_imag = real_gain * normals[1]
    delay_diag = (1.0 + damping) * (real_gain * real_gain + imag_gain * imag_gain) * normals[
        2
    ] + 1.0
    step_delay = (diagonal * normals[5] - cross_real * normals[3] - cross_imag * normals[4]) / (
        diagonal * delay_diag - cross_real * cross_real - cross_imag * cross_imag
    )
    step_real = (normals[3] - cross_real * step_delay) / diagonal
    step_imag = (normals[4] - cross_imag * step_delay) / diagonal
    return jnp.stack([real_gain + step_real, imag_gain + step_imag, delay + step_delay])


def shards(visibility, uv_coords, source_lm, source_flux, avg_factor, station_pairs, slot_owner):
    pair_corr = visibility.shape[0]
    slot_count = visibility.shape[2]
    chan_local = visibility.shape[3]
    base_count = visibility.shape[4]
    ch_count = lax.axis_size("ch")
    chan_total = chan_local * ch_count
    slot_local = slot_count // ch_count
    ch_position = lax.axis_index("ch")
    first_pol = lax.axis_index("pol")
    frequency = 0.5 + (jnp.arange(chan_total, dtype=jnp.float32) + 0.5) / chan_total
    frequency_local = lax.dynamic_slice_in_dim(frequency, ch_position * chan_local, chan_local, 0)
    slot_order = owner_slots(slot_owner)
    row_weights = jnp.take(averaging_weights(avg_factor, slot_count), slot_order, axis=0)

    def data_slot(slot_number):
        return lax.dynamic_index_in_dim(visibility, slot_number, 2, keepdims=False)

    def model_local(slot_number):
        uv_slot = lax.dynamic_index_in_dim(uv_coords, slot_number, 1, keepdims=False)
        return predict_slot(uv_slot, source_lm, source_flux, frequency_local, SRC_BLOCK)

    local_shape = (pair_corr, 2, slot_count, chan_local, base_count)
    data_rows = averaged_rows(row_weights, data_slot, local_shape)
    model_rows = averaged_rows(row_weights, model_local, local_shape)
    data_own, model_own = (
        lax.all_to_all(data_rows, "ch", split_axis=2, concat_axis=3, tiled=True),
        lax.all_to_all(model_rows, "ch", split_axis=2, concat_axis=3, tiled=True),
    )
    first_station = station_pairs[0]
    second_station = station_pairs[1]
    station_index = jnp.arange(STATIONS, dtype=jnp.int32)
    first_hot = (first_station[:, None] == station_index[None, :]).astype(jnp.float32)
    second_hot = (second_station[:, None] == station_index[None, :]).astype(jnp.float32)
    ones_part = jnp.ones((2, slot_local, STATIONS), jnp.float32)
    zero_part = jnp.zeros((2, slot_local, STATIONS), jnp.float32)
    gains = jnp.stack([ones_part, zero_part, zero_part])
    for iteration in range(ITERS):
        pieces = model_residual(
            data_own, model_own, gains, first_station, second_station, first_pol, frequency
        )
        terms = normal_terms(pieces, first_hot, second_hot, first_pol)
        normals = lax.psum(terms, ("bl", "pol"))
        gains = gain_update(gains, normals)
    pieces = model_residual(
        data_own, model_own, gains, first_station, second_station, first_pol, frequency
    )
    residual = jnp.stack([pieces[0], pieces[1]], axis=1)
    return (residual, gains)


def solution(mesh):
    placed = (
        P("pol", None, None, "ch", ("grp", "bl")),
        P(None, None, ("grp", "bl")),
        P(),
        P("pol", None),
        P(("grp", "bl")),
        P(None, ("grp", "bl")),
        P(),
    )
    return jax.shard_map(
        shards,
        mesh=mesh,
        in_specs=placed,
        out_specs=(P("pol", None, "ch", None, ("grp", "bl")), P(None, None, "ch", "grp")),
        check_vma=False,
    )
```

profile of v0, /device:TPU:0, one launch (start us, length us, event | category | flops | bytes accessed | tf_op | source)
XLA Modules:
  0.0 263.4 jit_solution(17737705359771054192)
XLA Ops:
  0.6 0.7 fusion.96
  1.4 0.7 fusion.121
  2.2 0.8 and_select_fusion
  3.7 126.9 %while.57 = (s32[]{:T(128)}, f32[2,2,2,192,128]{4,3,2,1,0:T(8,128)S(1)}, f32[2,2,128]{2,0,1:T(2,128)S(1)}, f32[2,64]{1,0:T(2,128)}, f32[2,2,128]{2,1,0:T(2,128)}...) while((s32[]{:T(128)}, ...), condition=%wide.region_6.9_spmd.clone, body=%wide.region_3.8_spmd.clone.sunk | while | flops 20570312 | bytes 4405188 | solution.py:55
  3.7 0.7 fusion.130
  4.4 0.8 slice_bitcast_fusion.5
  5.3 61.6 %while.58 = (s32[]{:T(128)}, f32[2,2,192,128]{3,0,2,1:T(2,128)S(1)}, f32[2,64]{1,0:T(2,128)}, f32[192]{0:T(256)S(1)}, f32[64,128]{1,0:T(8,128)S(1)}, /*index=5*/s32[]{:T(128)}, s32[]{:T(128)}, s32[]{:T(128)}, s32[]{:T(128)}) while((s32[]{:T(128)}, f32[2,2,192,128]{3,0,2,1:T(2,128)S(1)}, f32[2,64]{1,0:T(2,128)}, f32[192]{0:T(256)S(1)}, ...), condition=%wide.region_5.7_spmd.clone, body=%wide.region_4.6_spmd.clone.sunk | while | flops 19955908 | bytes 1611973 | solution.py:46
  5.3 7.8 %fusion.134 = f32[2,1,192,128]{3,0,2,1:T(2,128)S(1)} fusion(f32[16,128]{1,0:T(8,128)S(1)} %constant_dynamic-slice_fusion.4, f32[192]{0:T(256)S(1)} %broadcast_multiply_fusion.3, f32[2,64]{1,0:T(2,128)} %get-tuple-element.761, s32[]{:T(128)S(6)} %select_n.173), kind=kOutput, calls=%fused_computation.14.clone.1 | convolution fusion | flops 9830400 | bytes 206084 | tf_op jit(solution)/shard_map/while/body/eval_jaxpr/while/body/eval_jaxpr/ks,scb->kcb/dot_general | solution.py:42
  13.1 7.2 %fusion.133 = f32[2,1,192,128]{3,0,2,1:T(2,128)S(1)} fusion(f32[16,128]{1,0:T(8,128)S(1)} %constant_dynamic-slice_fusion.4, f32[192]{0:T(256)S(1)} %broadcast_multiply_fusion.3, f32[2,64]{1,0:T(2,128)S(1)} %copy-done.3, s32[]{:T(128)S(6)} %select_n.173), kind=kOutput, calls=%fused_computation.13.clone.1 | convolution fusion | flops 9830400 | bytes 206084 | tf_op jit(solution)/shard_map/while/body/eval_jaxpr/while/body/eval_jaxpr/ks,scb->kcb/dot_general | solution.py:43
  20.7 7.8 %fusion.134 = f32[2,1,192,128]{3,0,2,1:T(2,128)S(1)} fusion(f32[16,128]{1,0:T(8,128)S(1)} %constant_dynamic-slice_fusion.4, f32[192]{0:T(256)S(1)} %broadcast_multiply_fusion.3, f32[2,64]{1,0:T(2,128)} %get-tuple-element.761, s32[]{:T(128)S(6)} %select_n.173), kind=kOutput, calls=%fused_computation.14.clone.1 | convolution fusion | flops 9830400 | bytes 206084 | tf_op jit(solution)/shard_map/while/body/eval_jaxpr/while/body/eval_jaxpr/ks,scb->kcb/dot_general | solution.py:42
  28.5 7.2 %fusion.133 = f32[2,1,192,128]{3,0,2,1:T(2,128)S(1)} fusion(f32[16,128]{1,0:T(8,128)S(1)} %constant_dynamic-slice_fusion.4, f32[192]{0:T(256)S(1)} %broadcast_multiply_fusion.3, f32[2,64]{1,0:T(2,128)S(1)} %copy-done.3, s32[]{:T(128)S(6)} %select_n.173), kind=kOutput, calls=%fused_computation.13.clone.1 | convolution fusion | flops 9830400 | bytes 206084 | tf_op jit(solution)/shard_map/while/body/eval_jaxpr/while/body/eval_jaxpr/ks,scb->kcb/dot_general | solution.py:43
  36.1 7.8 %fusion.134 = f32[2,1,192,128]{3,0,2,1:T(2,128)S(1)} fusion(f32[16,128]{1,0:T(8,128)S(1)} %constant_dynamic-slice_fusion.4, f32[192]{0:T(256)S(1)} %broadcast_multiply_fusion.3, f32[2,64]{1,0:T(2,128)} %get-tuple-element.761, s32[]{:T(128)S(6)} %select_n.173), kind=kOutput, calls=%fused_computation.14.clone.1 | convolution fusion | flops 9830400 | bytes 206084 | tf_op jit(solution)/shard_map/while/body/eval_jaxpr/while/body/eval_jaxpr/ks,scb->kcb/dot_general | solution.py:42
  43.9 7.2 %fusion.133 = f32[2,1,192,128]{3,0,2,1:T(2,128)S(1)} fusion(f32[16,128]{1,0:T(8,128)S(1)} %constant_dynamic-slice_fusion.4, f32[192]{0:T(256)S(1)} %broadcast_multiply_fusion.3, f32[2,64]{1,0:T(2,128)S(1)} %copy-done.3, s32[]{:T(128)S(6)} %select_n.173), kind=kOutput, calls=%fused_computation.13.clone.1 | convolution fusion | flops 9830400 | bytes 206084 | tf_op jit(solution)/shard_map/while/body/eval_jaxpr/while/body/eval_jaxpr/ks,scb->kcb/dot_general | solution.py:43
  51.5 7.8 %fusion.134 = f32[2,1,192,128]{3,0,2,1:T(2,128)S(1)} fusion(f32[16,128]{1,0:T(8,128)S(1)} %constant_dynamic-slice_fusion.4, f32[192]{0:T(256)S(1)} %broadcast_multiply_fusion.3, f32[2,64]{1,0:T(2,128)} %get-tuple-element.761, s32[]{:T(128)S(6)} %select_n.173), kind=kOutput, calls=%fused_computation.14.clone.1 | convolution fusion | flops 9830400 | bytes 206084 | tf_op jit(solution)/shard_map/while/body/eval_jaxpr/while/body/eval_jaxpr/ks,scb->kcb/dot_general | solution.py:42
  59.3 7.2 %fusion.133 = f32[2,1,192,128]{3,0,2,1:T(2,128)S(1)} fusion(f32[16,128]{1,0:T(8,128)S(1)} %constant_dynamic-slice_fusion.4, f32[192]{0:T(256)S(1)} %broadcast_multiply_fusion.3, f32[2,64]{1,0:T(2,128)S(1)} %copy-done.3, s32[]{:T(128)S(6)} %select_n.173), kind=kOutput, calls=%fused_computation.13.clone.1 | convolution fusion | flops 9830400 | bytes 206084 | tf_op jit(solution)/shard_map/while/body/eval_jaxpr/while/body/eval_jaxpr/ks,scb->kcb/dot_general | solution.py:43
  67.2 0.7 fusion.130
  67.9 0.8 slice_bitcast_fusion.5
  68.7 61.6 %while.58 = (s32[]{:T(128)}, f32[2,2,192,128]{3,0,2,1:T(2,128)S(1)}, f32[2,64]{1,0:T(2,128)}, f32[192]{0:T(256)S(1)}, f32[64,128]{1,0:T(8,128)S(1)}, /*index=5*/s32[]{:T(128)}, s32[]{:T(128)}, s32[]{:T(128)}, s32[]{:T(128)}) while((s32[]{:T(128)}, f32[2,2,192,128]{3,0,2,1:T(2,128)S(1)}, f32[2,64]{1,0:T(2,128)}, f32[192]{0:T(256)S(1)}, ...), condition=%wide.region_5.7_spmd.clone, body=%wide.region_4.6_spmd.clone.sunk | while | flops 19955908 | bytes 1611973 | solution.py:46
  68.8 7.8 %fusion.134 = f32[2,1,192,128]{3,0,2,1:T(2,128)S(1)} fusion(f32[16,128]{1,0:T(8,128)S(1)} %constant_dynamic-slice_fusion.4, f32[192]{0:T(256)S(1)} %broadcast_multiply_fusion.3, f32[2,64]{1,0:T(2,128)} %get-tuple-element.761, s32[]{:T(128)S(6)} %select_n.173), kind=kOutput, calls=%fused_computation.14.clone.1 | convolution fusion | flops 9830400 | bytes 206084 | tf_op jit(solution)/shard_map/while/body/eval_jaxpr/while/body/eval_jaxpr/ks,scb->kcb/dot_general | solution.py:42
  76.6 7.2 %fusion.133 = f32[2,1,192,128]{3,0,2,1:T(2,128)S(1)} fusion(f32[16,128]{1,0:T(8,128)S(1)} %constant_dynamic-slice_fusion.4, f32[192]{0:T(256)S(1)} %broadcast_multiply_fusion.3, f32[2,64]{1,0:T(2,128)S(1)} %copy-done.3, s32[]{:T(128)S(6)} %select_n.173), kind=kOutput, calls=%fused_computation.13.clone.1 | convolution fusion | flops 9830400 | bytes 206084 | tf_op jit(solution)/shard_map/while/body/eval_jaxpr/while/body/eval_jaxpr/ks,scb->kcb/dot_general | solution.py:43
  84.2 7.8 %fusion.134 = f32[2,1,192,128]{3,0,2,1:T(2,128)S(1)} fusion(f32[16,128]{1,0:T(8,128)S(1)} %constant_dynamic-slice_fusion.4, f32[192]{0:T(256)S(1)} %broadcast_multiply_fusion.3, f32[2,64]{1,0:T(2,128)} %get-tuple-element.761, s32[]{:T(128)S(6)} %select_n.173), kind=kOutput, calls=%fused_computation.14.clone.1 | convolution fusion | flops 9830400 | bytes 206084 | tf_op jit(solution)/shard_map/while/body/eval_jaxpr/while/body/eval_jaxpr/ks,scb->kcb/dot_general | solution.py:42
  92.0 7.2 %fusion.133 = f32[2,1,192,128]{3,0,2,1:T(2,128)S(1)} fusion(f32[16,128]{1,0:T(8,128)S(1)} %constant_dynamic-slice_fusion.4, f32[192]{0:T(256)S(1)} %broadcast_multiply_fusion.3, f32[2,64]{1,0:T(2,128)S(1)} %copy-done.3, s32[]{:T(128)S(6)} %select_n.173), kind=kOutput, calls=%fused_computation.13.clone.1 | convolution fusion | flops 9830400 | bytes 206084 | tf_op jit(solution)/shard_map/while/body/eval_jaxpr/while/body/eval_jaxpr/ks,scb->kcb/dot_general | solution.py:43
  99.6 7.8 %fusion.134 = f32[2,1,192,128]{3,0,2,1:T(2,128)S(1)} fusion(f32[16,128]{1,0:T(8,128)S(1)} %constant_dynamic-slice_fusion.4, f32[192]{0:T(256)S(1)} %broadcast_multiply_fusion.3, f32[2,64]{1,0:T(2,128)} %get-tuple-element.761, s32[]{:T(128)S(6)} %select_n.173), kind=kOutput, calls=%fused_computation.14.clone.1 | convolution fusion | flops 9830400 | bytes 206084 | tf_op jit(solution)/shard_map/while/body/eval_jaxpr/while/body/eval_jaxpr/ks,scb->kcb/dot_general | solution.py:42
  107.4 7.2 %fusion.133 = f32[2,1,192,128]{3,0,2,1:T(2,128)S(1)} fusion(f32[16,128]{1,0:T(8,128)S(1)} %constant_dynamic-slice_fusion.4, f32[192]{0:T(256)S(1)} %broadcast_multiply_fusion.3, f32[2,64]{1,0:T(2,128)S(1)} %copy-done.3, s32[]{:T(128)S(6)} %select_n.173), kind=kOutput, calls=%fused_computation.13.clone.1 | convolution fusion | flops 9830400 | bytes 206084 | tf_op jit(solution)/shard_map/while/body/eval_jaxpr/while/body/eval_jaxpr/ks,scb->kcb/dot_general | solution.py:43
  115.0 7.8 %fusion.134 = f32[2,1,192,128]{3,0,2,1:T(2,128)S(1)} fusion(f32[16,128]{1,0:T(8,128)S(1)} %constant_dynamic-slice_fusion.4, f32[192]{0:T(256)S(1)} %broadcast_multiply_fusion.3, f32[2,64]{1,0:T(2,128)} %get-tuple-element.761, s32[]{:T(128)S(6)} %select_n.173), kind=kOutput, calls=%fused_computation.14.clone.1 | convolution fusion | flops 9830400 | bytes 206084 | tf_op jit(solution)/shard_map/while/body/eval_jaxpr/while/body/eval_jaxpr/ks,scb->kcb/dot_general | solution.py:42
  122.8 7.2 %fusion.133 = f32[2,1,192,128]{3,0,2,1:T(2,128)S(1)} fusion(f32[16,128]{1,0:T(8,128)S(1)} %constant_dynamic-slice_fusion.4, f32[192]{0:T(256)S(1)} %broadcast_multiply_fusion.3, f32[2,64]{1,0:T(2,128)S(1)} %copy-done.3, s32[]{:T(128)S(6)} %select_n.173), kind=kOutput, calls=%fused_computation.13.clone.1 | convolution fusion | flops 9830400 | bytes 206084 | tf_op jit(solution)/shard_map/while/body/eval_jaxpr/while/body/eval_jaxpr/ks,scb->kcb/dot_general | solution.py:43
  130.6 0.9 copy.189
  131.6 4.3 %all-to-all-start.1 = ((f32[2,2,2,192,128]{4,3,1,0,2:T(8,128)}), f32[2,2,2,192,128]{4,3,1,0,2:T(8,128)S(1)}, u32[]{:S(2)}, u32[]{:S(2)}) async-start(f32[2,2,2,192,128]{4,3,1,0,2:T(8,128)} %copy.189), calls=%async_computation.1 | async-start | bytes 1572864 | tf_op jit(solution)/shard_map/all_to_all | solution.py:180
  136.0 0.7 while.55
  136.6 1.8 gather_fusion.2
  139.5 0.9 copy.184
  140.7 6.8 %all-to-all-done.1 = f32[2,2,2,192,128]{4,3,1,0,2:T(8,128)S(1)} async-done(((f32[2,2,2,192,128]{4,3,1,0,2:T(8,128)}), f32[2,2,2,192,128]{4,3,1,0,2:T(8,128)S(1)}, u32[]{:S(2)}, u32[]{:S(2)}) %all-to-all-start.1) | async-done | bytes 786464 | tf_op jit(solution)/shard_map/all_to_all | solution.py:180
  147.5 3.5 %all-to-all-start = ((f32[2,2,2,192,128]{4,3,1,0,2:T(8,128)}), f32[2,2,2,192,128]{4,3,1,0,2:T(8,128)S(1)}, u32[]{:S(2)}, u32[]{:S(2)}) async-start(f32[2,2,2,192,128]{4,3,1,0,2:T(8,128)} %copy.184), calls=%async_computation | async-start | bytes 1572864 | tf_op jit(solution)/shard_map/all_to_all | solution.py:179
  151.6 9.9 %all-to-all-done = f32[2,2,2,192,128]{4,3,1,0,2:T(8,128)S(1)} async-done(((f32[2,2,2,192,128]{4,3,1,0,2:T(8,128)}), f32[2,2,2,192,128]{4,3,1,0,2:T(8,128)S(1)}, u32[]{:S(2)}, u32[]{:S(2)}) %all-to-all-start) | async-done | bytes 786464 | tf_op jit(solution)/shard_map/all_to_all | solution.py:179
  161.6 2.0 subtract_multiply_fusion.2
  165.0 27.0 %psum.21 = f32[6,2,1,512]{3,1,0,2:T(2,128)S(1)} all-reduce(f32[6,2,1,512]{3,1,0,2:T(2,128)S(1)} %fusion.58), channel_id=1, replica_groups=mesh['grp'=2,'bl'=4,'ch'=2,'pol'=2] {'bl','pol'}, use_global_device_ids=true, to_apply=%region_19.22 | all-reduce | flops 6144 | bytes 49152 | tf_op jit(solution)/shard_map/psum | solution.py:195
  192.2 0.7 gather_fusion.3
  193.4 0.7 gather_fusion.4
  195.0 2.0 subtract_multiply_fusion.1
  198.3 26.1 %psum.22 = f32[6,2,1,512]{3,1,2,0:T(2,128)S(1)} all-reduce(f32[6,2,1,512]{3,1,2,0:T(2,128)S(1)} %fusion.57), channel_id=1, replica_groups=mesh['grp'=2,'bl'=4,'ch'=2,'pol'=2] {'bl','pol'}, use_global_device_ids=true, to_apply=%region_32.36 | all-reduce | flops 6144 | bytes 49152 | tf_op jit(solution)/shard_map/psum | solution.py:195
  224.8 0.7 gather_fusion.5
  226.0 0.7 gather_fusion.6
  227.5 2.0 subtract_multiply_fusion
  230.9 26.0 %psum.23 = f32[6,2,1,512]{3,1,2,0:T(2,128)S(1)} all-reduce(f32[6,2,1,512]{3,1,2,0:T(2,128)S(1)} %fusion.56), channel_id=1, replica_groups=mesh['grp'=2,'bl'=4,'ch'=2,'pol'=2] {'bl','pol'}, use_global_device_ids=true, to_apply=%region_45.49 | all-reduce | flops 6144 | bytes 49152 | tf_op jit(solution)/shard_map/psum | solution.py:195
  257.8 0.7 gather_fusion.7
  259.0 0.7 gather_fusion.8
  260.5 1.9 subtract_subtract_fusion
  262.5 0.9 maximum_bitcast_fusion
  (182 shorter events, 16.2 us)
Async XLA Ops:
  5.3 7.9 %copy-start.3 = (f32[2,64]{1,0:T(2,128)S(1)}, f32[2,64]{1,0:T(2,128)}, u32[]{:S(2)}) copy-start(f32[2,64]{1,0:T(2,128)} %get-tuple-element.761) | copy-start | bytes 1540 | tf_op jit(solution)/shard_map/while/body/eval_jaxpr/while
  20.7 7.9 %copy-start.3 = (f32[2,64]{1,0:T(2,128)S(1)}, f32[2,64]{1,0:T(2,128)}, u32[]{:S(2)}) copy-start(f32[2,64]{1,0:T(2,128)} %get-tuple-element.761) | copy-start | bytes 1540 | tf_op jit(solution)/shard_map/while/body/eval_jaxpr/while
  36.1 7.9 %copy-start.3 = (f32[2,64]{1,0:T(2,128)S(1)}, f32[2,64]{1,0:T(2,128)}, u32[]{:S(2)}) copy-start(f32[2,64]{1,0:T(2,128)} %get-tuple-element.761) | copy-start | bytes 1540 | tf_op jit(solution)/shard_map/while/body/eval_jaxpr/while
  51.5 7.9 %copy-start.3 = (f32[2,64]{1,0:T(2,128)S(1)}, f32[2,64]{1,0:T(2,128)}, u32[]{:S(2)}) copy-start(f32[2,64]{1,0:T(2,128)} %get-tuple-element.761) | copy-start | bytes 1540 | tf_op jit(solution)/shard_map/while/body/eval_jaxpr/while
  68.7 7.9 %copy-start.3 = (f32[2,64]{1,0:T(2,128)S(1)}, f32[2,64]{1,0:T(2,128)}, u32[]{:S(2)}) copy-start(f32[2,64]{1,0:T(2,128)} %get-tuple-element.761) | copy-start | bytes 1540 | tf_op jit(solution)/shard_map/while/body/eval_jaxpr/while
  84.1 7.9 %copy-start.3 = (f32[2,64]{1,0:T(2,128)S(1)}, f32[2,64]{1,0:T(2,128)}, u32[]{:S(2)}) copy-start(f32[2,64]{1,0:T(2,128)} %get-tuple-element.761) | copy-start | bytes 1540 | tf_op jit(solution)/shard_map/while/body/eval_jaxpr/while
  99.5 7.9 %copy-start.3 = (f32[2,64]{1,0:T(2,128)S(1)}, f32[2,64]{1,0:T(2,128)}, u32[]{:S(2)}) copy-start(f32[2,64]{1,0:T(2,128)} %get-tuple-element.761) | copy-start | bytes 1540 | tf_op jit(solution)/shard_map/while/body/eval_jaxpr/while
  114.9 7.9 %copy-start.3 = (f32[2,64]{1,0:T(2,128)S(1)}, f32[2,64]{1,0:T(2,128)}, u32[]{:S(2)}) copy-start(f32[2,64]{1,0:T(2,128)} %get-tuple-element.761) | copy-start | bytes 1540 | tf_op jit(solution)/shard_map/while/body/eval_jaxpr/while
  131.6 4.3 %copy-start.2 = (s32[2,128]{1,0:T(2,128)S(1)}, s32[2,128]{1,0:T(2,128)}, u32[]{:S(2)}) copy-start(s32[2,128]{1,0:T(2,128)} %param.24) | copy-start | bytes 3076
  131.6 4.4 %copy-start = (f32[2,2,2,192,128]{4,3,2,1,0:T(8,128)S(1)}, f32[2,2,2,192,128]{4,3,2,1,0:T(8,128)}, u32[]{:S(2)}) copy-start(f32[2,2,2,192,128]{4,3,2,1,0:T(8,128)} %param.19) | copy-start | bytes 2359300
  131.6 15.9 %all-to-all-start.1 = ((f32[2,2,2,192,128]{4,3,1,0,2:T(8,128)}), f32[2,2,2,192,128]{4,3,1,0,2:T(8,128)S(1)}, u32[]{:S(2)}, u32[]{:S(2)}) async-start(f32[2,2,2,192,128]{4,3,1,0,2:T(8,128)} %copy.189), calls=%async_computation.1 | async-start | bytes 1572864 | tf_op jit(solution)/shard_map/all_to_all | solution.py:180
  135.9 2.7 %copy-start.1 = (f32[3,2,1,512]{0,3,2,1:T(8,128)S(1)}, f32[3,2,1,512]{0,3,2,1:T(8,128)}, u32[]{:S(2)}) copy-start(f32[3,2,1,512]{0,3,2,1:T(8,128)} %constant.178.clone.1) | copy-start | bytes 36868
  147.5 14.0 %all-to-all-start = ((f32[2,2,2,192,128]{4,3,1,0,2:T(8,128)}), f32[2,2,2,192,128]{4,3,1,0,2:T(8,128)S(1)}, u32[]{:S(2)}, u32[]{:S(2)}) async-start(f32[2,2,2,192,128]{4,3,1,0,2:T(8,128)} %copy.184), calls=%async_computation | async-start | bytes 1572864 | tf_op jit(solution)/shard_map/all_to_all | solution.py:179
where the time goes:
time: 264 us; the launch traced here: 263 us
  matrix products  121 us (46%)
  blocking collectives  79.1 us (30%)
  other arithmetic  18.6 us (7%)
  local copies, waits for them, and re-layouts  17.8 us (7%)
  waiting for transfers between devices  16.7 us (6%)
  starting transfers between devices  7.87 us (3%)
    psum x3, blocking collectives, shards(): normals = lax.psum(terms, ('bl', 'pol'))  79.1 us
    dot_general x8, matrix products, add_block(): jnp.einsum('ks,scb->kcb', flux_block, jnp.cos(phase_angle), precision=hig...  62.5 us
    dot_general x8, matrix products, add_block(): jnp.einsum('ks,scb->kcb', flux_block, jnp.sin(phase_angle), precision=hig...  57.3 us
    all_to_all x1, waiting for transfers between devices, shards(): lax.all_to_all(data_rows, 'ch', split_axis=2, concat_axis=3, tiled=True)  9.92 us
    all_to_all x1, waiting for transfers between devices, shards(): lax.all_to_all(model_rows, 'ch', split_axis=2, concat_axis=3, tiled=True)  6.76 us
    mul x3, other arithmetic, normal_terms(): angular * pred_cross  5.96 us
  transfers between devices with their start and end apart: 2, of which 2 were waited for; matrix products, arithmetic and copies ran while one was open for 2% of the time, Pallas kernels for 0%

commit v1 on v0

v1 whole, which is shorter than its diff:
```python
import functools

import jax
import jax.numpy as jnp
from jax import lax
from jax.experimental import pallas as pl
from jax.experimental.pallas import tpu as pltpu
from jax.sharding import PartitionSpec as P

ITERS = 3
LANES = 128
TILE = 4
damping = 1.0
two_pi = 6.283185307179586
MESH = pl.DeviceIdType.MESH

SIN_COEF = (
    3.141592653589793,
    -5.16771278004997,
    2.550164039877345,
    -0.5992645293207921,
    0.08214588661112823,
    -0.00737043094571435,
)
COS_COEF = (
    1.0,
    -4.934802200544679,
    4.058712126416768,
    -1.3352627688545893,
    0.2353306303588935,
    -0.02580689139001406,
    0.0019295743094039231,
)


def sincos_turns(turns):
    part = turns - jnp.floor(turns + 0.5)
    sq = part * part
    sin_half = jnp.full_like(sq, SIN_COEF[-1])
    for coef in SIN_COEF[-2::-1]:
        sin_half = sin_half * sq + coef
    sin_half = sin_half * part
    cos_half = jnp.full_like(sq, COS_COEF[-1])
    for coef in COS_COEF[-2::-1]:
        cos_half = cos_half * sq + coef
    twice = sin_half + sin_half
    return twice * cos_half, 1.0 - twice * sin_half


def split3(value):
    high = value.astype(jnp.bfloat16)
    rest = value - high.astype(jnp.float32)
    mid = rest.astype(jnp.bfloat16)
    low = (rest - mid.astype(jnp.float32)).astype(jnp.bfloat16)
    return jnp.concatenate([high, mid, low], axis=0)


def kernel(
    sizes,
    vis,
    uv,
    lm,
    flux,
    factor,
    pairs,
    owner,
    res_out,
    gains_out,
    vbuf,
    sbuf,
    model,
    geo,
    ftab,
    dtab,
    xtab,
    psend,
    pall,
    mall,
    yall,
    onehot,
    terms,
    gathered,
    v_send,
    v_recv,
    p_send,
    p_recv,
    m_send,
    m_recv,
    y_send,
    y_recv,
):
    ch_count, bl_count, pol_count, slots, chan_local, chans, sources, stations = sizes
    ch = lax.axis_index("ch")
    bl = lax.axis_index("bl")
    pol = lax.axis_index("pol")
    group = bl_count * pol_count
    me = bl * pol_count + pol
    half = chans // 16
    base_all = bl_count * LANES

    def ch_peer(step):
        return lax.rem(ch + step, ch_count)

    def group_peer(step):
        other = lax.rem(me + step, group)
        return {"bl": other // pol_count, "pol": lax.rem(other, pol_count)}

    barrier = pltpu.get_barrier_semaphore()
    for step in range(1, ch_count):
        pl.semaphore_signal(
            barrier, inc=1, device_id={"ch": ch_peer(step)}, device_id_type=MESH
        )
    for step in range(1, group):
        pl.semaphore_signal(barrier, inc=1, device_id=group_peer(step), device_id_type=MESH)

    fac = factor[...]
    inverse = jnp.zeros(fac.shape, jnp.float32)
    power = 1
    while power <= slots:
        inverse = jnp.where(fac == power, jnp.float32(1.0 / power), inverse)
        power *= 2

    def weight_rows(position):
        slot = jnp.int32(0)
        for s in range(slots):
            slot = slot + jnp.where(owner[s] == position, jnp.int32(s), jnp.int32(0))
        return [
            jnp.where(jnp.bitwise_xor(slot, jnp.int32(t)) < fac, inverse, 0.0)
            for t in range(slots)
        ]

    def averaged(rows, k, r):
        total = rows[0] * vis[k, r, 0]
        for t in range(1, slots):
            total = total + rows[t] * vis[k, r, t]
        return total

    for step in range(1, ch_count):
        rows = weight_rows(ch_peer(step))
        for k in range(2):
            for r in range(2):
                sbuf[step - 1, k, r] = averaged(rows, k, r)
    own_rows = weight_rows(ch)
    own_span = pl.ds(pl.multiple_of(ch * chan_local, 8), chan_local)
    for i in range(2):
        psend[pl.ds(i, 1), :] = pairs[pl.ds(i, 1), :]
    psend[pl.ds(2, 6), :] = jnp.zeros((6, LANES), jnp.int32)

    pl.semaphore_wait(barrier, ch_count - 1 + group - 1)

    v_copies = []
    for step in range(1, ch_count):
        copy = pltpu.make_async_remote_copy(
            src_ref=sbuf.at[step - 1],
            dst_ref=vbuf.at[:, :, own_span, :],
            send_sem=v_send.at[step - 1],
            recv_sem=v_recv.at[step - 1],
            device_id={"ch": ch_peer(step)},
            device_id_type=MESH,
        )
        copy.start()
        v_copies.append(copy)
    p_copies = []
    for step in range(1, bl_count):
        copy = pltpu.make_async_remote_copy(
            src_ref=psend,
            dst_ref=pall.at[bl],
            send_sem=p_send.at[step - 1],
            recv_sem=p_recv.at[step - 1],
            device_id={"bl": lax.rem(bl + step, bl_count)},
            device_id_type=MESH,
        )
        copy.start()
        p_copies.append(copy)
    pall[bl] = psend[...]
    for k in range(2):
        for r in range(2):
            vbuf[k, r, own_span, :] = averaged(own_rows, k, r)

    def geo_row(s, _):
        for t in range(slots):
            geo[pl.ds(t * sources + s, 1), :] = -(
                lm[0, s] * uv[0, pl.ds(t, 1), :] + lm[1, s] * uv[1, pl.ds(t, 1), :]
            )
        return 0

    lax.fori_loop(0, sources, geo_row, 0, unroll=8)

    def offset_rows(block, _):
        span = pl.ds(pl.multiple_of(block * 32, 32), 32)
        sin_h, cos_h = sincos_turns(geo[span, :] * jnp.float32(4.0 / chans))
        cos_f = cos_h * cos_h - sin_h * sin_h
        sin_f = 2.0 * sin_h * cos_h
        for d in range(half):
            dtab[d, 0, span, :] = cos_h
            dtab[d, 1, span, :] = sin_h
            cos_h, sin_h = cos_h * cos_f - sin_h * sin_f, sin_h * cos_f + cos_h * sin_f
        return 0

    lax.fori_loop(0, slots * sources // 32, offset_rows, 0)

    sub = lax.broadcasted_iota(jnp.int32, (8, LANES), 0).astype(jnp.float32)
    freq_c = 0.5 + (sub + jnp.float32(4 * (chans // 8 - 1) + 0.5)) / chans
    omega_c = two_pi * freq_c
    omega_step = jnp.float32(two_pi * 8.0 / chans)

    for t in range(slots):
        wide = jnp.broadcast_to(own_rows[t], (8, LANES))

        def centre(s, _, t=t, wide=wide):
            row = t * sources + s
            sin_c, cos_c = sincos_turns(geo[pl.ds(row, 1), :] * freq_c)
            sin_c = sin_c * wide
            cos_c = cos_c * wide
            span = pl.ds(pl.multiple_of(row * 8, 8), 8)
            for k in range(2):
                ftab[k, 0, span, :] = flux[k, s] * cos_c
                ftab[k, 1, span, :] = flux[k, s] * sin_c
            return 0

        lax.fori_loop(0, sources, centre, 0, unroll=4)

    zero = jnp.zeros((8, LANES), jnp.float32)
    moments = [[zero, zero, zero] for _ in range(2)]
    for first in range(0, half, TILE):
        count = min(TILE, half - first)

        def add_source(row, acc, first=first, count=count):
            span = pl.ds(pl.multiple_of(row * 8, 8), 8)
            fc = [ftab[k, 0, span, :] for k in range(2)]
            fs = [ftab[k, 1, span, :] for k in range(2)]
            out = []
            at = 0
            for d in range(count):
                cd = jnp.broadcast_to(dtab[first + d, 0, pl.ds(row, 1), :], (8, LANES))
                sd = jnp.broadcast_to(dtab[first + d, 1, pl.ds(row, 1), :], (8, LANES))
                for k in range(2):
                    out.append(acc[at] + fc[k] * cd)
                    out.append(acc[at + 1] + fs[k] * sd)
                    out.append(acc[at + 2] + fs[k] * cd)
                    out.append(acc[at + 3] + fc[k] * sd)
                    at += 4
            return tuple(out)

        acc = lax.fori_loop(
            0, slots * sources, add_source, (zero,) * (8 * count), unroll=4
        )
        for d in range(count):
            dist = jnp.float32(first + d + 0.5)
            up = pl.ds(8 * (half + first + d), 8)
            down = pl.ds(8 * (half - 1 - first - d), 8)
            for k in range(2):
                cc, ss, sc, cs = acc[(d * 2 + k) * 4 : (d * 2 + k) * 4 + 4]
                up_r, up_i, dn_r, dn_i = cc - ss, sc + cs, cc + ss, sc - cs
                model[k, 0, up, :] = up_r
                model[k, 1, up, :] = up_i
                model[k, 0, down, :] = dn_r
                model[k, 1, down, :] = dn_i
                up_p = up_r * up_r + up_i * up_i
                dn_p = dn_r * dn_r + dn_i * dn_i
                both = up_p + dn_p
                moments[k][0] = moments[k][0] + both
                moments[k][1] = moments[k][1] + dist * (up_p - dn_p)
                moments[k][2] = moments[k][2] + (dist * dist) * both

    def fold(value):
        return jnp.sum(value, axis=0, keepdims=True)

    for k in range(2):
        a0, a1, a2 = moments[k]
        mall[me, pl.ds(k, 1), :] = fold(a0)
        mall[me, pl.ds(2 + k, 1), :] = fold(omega_c * a0 + omega_step * a1)
        mall[me, pl.ds(4 + k, 1), :] = fold(
            omega_c * omega_c * a0
            + 2.0 * omega_step * omega_c * a1
            + omega_step * omega_step * a2
        )
    mall[me, pl.ds(6, 2), :] = jnp.zeros((2, LANES), jnp.float32)

    def spread(block, send_sem, recv_sem):
        copies = []
        for step in range(1, group):
            copy = pltpu.make_async_remote_copy(
                src_ref=block,
                dst_ref=block,
                send_sem=send_sem.at[step - 1],
                recv_sem=recv_sem.at[step - 1],
                device_id=group_peer(step),
                device_id_type=MESH,
            )
            copy.start()
            copies.append(copy)
        return copies

    m_copies = spread(mall.at[me], m_send, m_recv)

    for copy in p_copies:
        copy.wait()
    station = lax.broadcasted_iota(jnp.int32, (stations, LANES), 0)
    for b in range(bl_count):
        for i in range(2):
            hot = (station == pall[b, pl.ds(i, 1), :]).astype(jnp.float32)
            onehot[:, pl.ds(i * base_all + b * LANES, LANES)] = hot.astype(jnp.bfloat16)

    for copy in v_copies:
        copy.wait()

    for d in range(half):
        up = pl.ds(8 * (half + d), 8)
        down = pl.ds(8 * (half - 1 - d), 8)
        at = pl.ds(8 * d, 8)
        for k in range(2):
            halves = []
            for span in (up, down):
                m_r, m_i = model[k, 0, span, :], model[k, 1, span, :]
                v_r, v_i = vbuf[k, 0, span, :], vbuf[k, 1, span, :]
                halves.append((m_r * v_r + m_i * v_i, m_r * v_i - m_i * v_r))
            (u_r, u_i), (l_r, l_i) = halves
            xtab[k, 0, at, :] = u_r + l_r
            xtab[k, 1, at, :] = u_i + l_i
            xtab[k, 2, at, :] = u_r - l_r
            xtab[k, 3, at, :] = u_i - l_i

    own_first = pl.ds(pl.multiple_of(bl * LANES, LANES), LANES)
    own_second = pl.ds(pl.multiple_of(base_all + bl * LANES, LANES), LANES)
    dist_col = lax.broadcasted_iota(jnp.int32, (half, LANES), 0).astype(jnp.float32) + 0.5

    def own_gain(row):
        return jnp.where(
            pol == 0,
            gathered[pl.ds(row, 1), own_first],
            gathered[pl.ds(row + 1, 1), own_first],
        )

    def delay_tables(k):
        tau = own_gain(4) - gathered[pl.ds(4 + k, 1), own_second]
        sin_d, cos_d = sincos_turns(dist_col * (tau * jnp.float32(8.0 / chans)))
        sin_c, cos_c = sincos_turns(freq_c * tau)
        return sin_d, cos_d, sin_c, cos_c

    gains = (
        jnp.ones((2, stations), jnp.float32),
        jnp.zeros((2, stations), jnp.float32),
        jnp.zeros((2, stations), jnp.float32),
    )
    gathered[pl.ds(0, 2), :] = jnp.ones((2, 2 * base_all), jnp.float32)
    gathered[pl.ds(2, 14), :] = jnp.zeros((14, 2 * base_all), jnp.float32)
    terms[pl.ds(12, 4), :] = jnp.zeros((4, 2 * base_all), jnp.float32)

    for it in range(ITERS):
        for k in range(2):
            if it > 0:
                sin_d, cos_d, sin_c, cos_c = delay_tables(k)
            u_r, u_i, w_r, w_i = zero, zero, zero, zero
            for d in range(half):
                at = pl.ds(8 * d, 8)
                p_r, p_i = xtab[k, 0, at, :], xtab[k, 1, at, :]
                m_r, m_i = xtab[k, 2, at, :], xtab[k, 3, at, :]
                dist = jnp.float32(d + 0.5)
                if it > 0:
                    cd, sd = cos_d[d : d + 1, :], sin_d[d : d + 1, :]
                    u_r = u_r + (cd * p_r + sd * m_i)
                    u_i = u_i + (cd * p_i - sd * m_r)
                    cd, sd = dist * cd, dist * sd
                    w_r = w_r + (cd * m_r + sd * p_i)
                    w_i = w_i + (cd * m_i - sd * p_r)
                else:
                    u_r = u_r + p_r
                    u_i = u_i + p_i
                    w_r = w_r + dist * m_r
                    w_i = w_i + dist * m_i
            w_r = omega_c * u_r + omega_step * w_r
            w_i = omega_c * u_i + omega_step * w_i
            if it > 0:
                u_r, u_i = cos_c * u_r + sin_c * u_i, cos_c * u_i - sin_c * u_r
                w_r, w_i = cos_c * w_r + sin_c * w_i, cos_c * w_i - sin_c * w_r
            for n, value in enumerate((u_r, u_i, w_r, w_i)):
                yall[it, me, pl.ds(2 * n + k, 1), :] = fold(value)
        copies = spread(yall.at[it, me], y_send.at[it], y_recv.at[it])
        if it == 0:
            for copy in m_copies:
                copy.wait()
        for copy in copies:
            copy.wait()

        for b in range(bl_count):
            lane_1 = pl.ds(b * LANES, LANES)
            lane_2 = pl.ds(base_all + b * LANES, LANES)
            uj, wj = gathered[pl.ds(0, 2), lane_2], gathered[pl.ds(2, 2), lane_2]
            nj = uj * uj + wj * wj
            second = [jnp.zeros((2, LANES), jnp.float32)] * 6
            for p in range(pol_count):
                dev = b * pol_count + p
                ui, wi = gathered[pl.ds(p, 1), lane_1], gathered[pl.ds(2 + p, 1), lane_1]
                ni = ui * ui + wi * wi
                y0r, y0i, y1r, y1i = [yall[it, dev, pl.ds(2 * n, 2), :] for n in range(4)]
                p0, p1, p2 = [mall[dev, pl.ds(2 * n, 2), :] for n in range(3)]
                b_r = uj * y1r - wj * y1i
                b_i = uj * y1i + wj * y1r
                cross = ui * b_i - wi * b_r
                s0 = nj * p0
                first = (
                    s0,
                    nj * p1,
                    nj * p2,
                    uj * y0r - wj * y0i - ui * s0,
                    uj * y0i + wj * y0r - wi * s0,
                    cross,
                )
                for x in range(6):
                    terms[pl.ds(2 * x + p, 1), lane_1] = fold(first[x])
                t0 = ni * p0
                more = (
                    t0,
                    ni * p1,
                    ni * p2,
                    ui * y0r + wi * y0i - uj * t0,
                    -(ui * y0i - wi * y0r + wj * t0),
                    -cross,
                )
                second = [a + c for a, c in zip(second, more)]
            for x in range(6):
                terms[pl.ds(2 * x, 2), lane_2] = second[x]

        summed = lax.dot_general(
            split3(terms[...]),
            onehot[...],
            (((1,), (1,)), ((), ())),
            preferred_element_type=jnp.float32,
        )
        summed = summed[0:16] + summed[16:32] + summed[32:48]
        s0, s1, s2, g1, g2, g3 = [summed[2 * x : 2 * x + 2] for x in range(6)]
        u, w, tau = gains
        diagonal = (1.0 + damping) * s0 + 1.0
        cross_r = -w * s1
        cross_i = u * s1
        delay_diag = (1.0 + damping) * (u * u + w * w) * s2 + 1.0
        step_d = (diagonal * g3 - cross_r * g1 - cross_i * g2) / (
            diagonal * delay_diag - cross_r * cross_r - cross_i * cross_i
        )
        step_u = (g1 - cross_r * step_d) / diagonal
        step_w = (g2 - cross_i * step_d) / diagonal
        gains = (u + step_u, w + step_w, tau + step_d)

        rows = jnp.concatenate(
            list(gains) + [jnp.zeros((10, stations), jnp.float32)], axis=0
        )
        got = jnp.dot(split3(rows), onehot[...], preferred_element_type=jnp.float32)
        gathered[...] = got[0:16] + got[16:32] + got[32:48]

    for n in range(3):
        gains_out[n, :, 0, :] = gains[n]

    for k in range(2):
        sin_d, cos_d, sin_c, cos_c = delay_tables(k)
        ui, wi = own_gain(0), own_gain(2)
        uj, wj = gathered[pl.ds(k, 1), own_second], gathered[pl.ds(2 + k, 1), own_second]
        g_r = ui * uj + wi * wj
        g_i = wi * uj - ui * wj
        e_r = g_r * cos_c - g_i * sin_c
        e_i = g_r * sin_c + g_i * cos_c
        for d in range(half):
            cd, sd = cos_d[d : d + 1, :], sin_d[d : d + 1, :]
            c_r, c_i, s_r, s_i = e_r * cd, e_i * cd, e_r * sd, e_i * sd
            up = pl.ds(8 * (half + d), 8)
            down = pl.ds(8 * (half - 1 - d), 8)
            for span, f_r, f_i in (
                (up, c_r - s_i, c_i + s_r),
                (down, c_r + s_i, c_i - s_r),
            ):
                m_r, m_i = model[k, 0, span, :], model[k, 1, span, :]
                res_out[k, 0, 0, span, :] = vbuf[k, 0, span, :] - (f_r * m_r - f_i * m_i)
                res_out[k, 1, 0, span, :] = vbuf[k, 1, span, :] - (f_r * m_i + f_i * m_r)


def shards(
    stations, visibility, uv_coords, source_lm, source_flux, avg_factor, station_pairs, slot_owner
):
    ch_count = lax.axis_size("ch")
    bl_count = lax.axis_size("bl")
    pol_count = lax.axis_size("pol")
    slots, chan_local = visibility.shape[2], visibility.shape[3]
    chans = chan_local * ch_count
    sources = source_lm.shape[1]
    half = chans // 16
    group = bl_count * pol_count
    sizes = (ch_count, bl_count, pol_count, slots, chan_local, chans, sources, stations)
    f32 = jnp.float32
    vmem = pl.BlockSpec(memory_space=pltpu.VMEM)
    smem = pl.BlockSpec(memory_space=pltpu.SMEM)
    dma = pltpu.SemaphoreType.DMA
    return pl.pallas_call(
        functools.partial(kernel, sizes),
        out_shape=(
            jax.ShapeDtypeStruct((2, 2, 1, chans, LANES), f32),
            jax.ShapeDtypeStruct((3, 2, 1, stations), f32),
        ),
        in_specs=[vmem, vmem, smem, smem, vmem, vmem, smem],
        out_specs=(vmem, vmem),
        scratch_shapes=[
            pltpu.VMEM((2, 2, chans, LANES), f32),
            pltpu.VMEM((ch_count - 1, 2, 2, chan_local, LANES), f32),
            pltpu.VMEM((2, 2, chans, LANES), f32),
            pltpu.VMEM((slots * sources, LANES), f32),
            pltpu.VMEM((2, 2, slots * sources * 8, LANES), f32),
            pltpu.VMEM((half, 2, slots * sources, LANES), f32),
            pltpu.VMEM((2, 4, half * 8, LANES), f32),
            pltpu.VMEM((8, LANES), jnp.int32),
            pltpu.VMEM((bl_count, 8, LANES), jnp.int32),
            pltpu.VMEM((group, 8, LANES), f32),
            pltpu.VMEM((ITERS, group, 8, LANES), f32),
            pltpu.VMEM((stations, 2 * bl_count * LANES), jnp.bfloat16),
            pltpu.VMEM((16, 2 * bl_count * LANES), f32),
            pltpu.VMEM((16, 2 * bl_count * LANES), f32),
            dma((ch_count - 1,)),
            dma((ch_count - 1,)),
            dma((bl_count - 1,)),
            dma((bl_count - 1,)),
            dma((group - 1,)),
            dma((group - 1,)),
            dma((ITERS, group - 1)),
            dma((ITERS, group - 1)),
        ],
        compiler_params=pltpu.CompilerParams(
            collective_id=0, has_side_effects=True, vmem_limit_bytes=56 * 1024 * 1024
        ),
    )(
        visibility,
        uv_coords,
        source_lm,
        source_flux,
        avg_factor.reshape(1, -1),
        station_pairs,
        slot_owner,
    )


def solution(mesh):
    placed = (
        P("pol", None, None, "ch", ("grp", "bl")),
        P(None, None, ("grp", "bl")),
        P(),
        P("pol", None),
        P(("grp", "bl")),
        P(None, ("grp", "bl")),
        P(),
    )
    return jax.shard_map(
        functools.partial(shards, 512),
        mesh=mesh,
        in_specs=placed,
        out_specs=(P("pol", None, "ch", None, ("grp", "bl")), P(None, None, "ch", "grp")),
        check_vma=False,
    )
```

time: 264 us -> 35.5 us (0.13)
  matrix products: 121 us -> 0 us
  blocking collectives: 79.1 us -> 0 us
  Pallas kernels: 0 us -> 32 us
  other arithmetic: 18.6 us -> 0 us
  waiting for transfers between devices: 16.7 us -> 0 us
  local copies, waits for them, and re-layouts: 17.8 us -> 2.67 us
  starting transfers between devices: 7.87 us -> 0 us
    dot_general x22 -> x0, matrix products: 121 us -> none  [the longest x8 62.5 us: add_block(): jnp.einsum('ks,scb->kcb', flux_block, jnp.cos(phase_angle), precision=hig...]
    psum x3 -> x0, blocking collectives: 79.1 us -> none  [shards(): normals = lax.psum(terms, ('bl', 'pol'))]
    pallas_call x0 -> x1, Pallas kernels: none -> 32 us  [shards(): pl.pallas_call(functools.partial(kernel, sizes), out_shape=(jax.ShapeDtyp...]
    all_to_all x2 -> x0, waiting for transfers between devices: 16.7 us -> none  [the longest x1 9.92 us: shards(): lax.all_to_all(data_rows, 'ch', split_axis=2, concat_axis=3, tiled=True)]
    all_to_all x2 -> x0, starting transfers between devices: 7.87 us -> none  [the longest x1 4.34 us: shards(): lax.all_to_all(model_rows, 'ch', split_axis=2, concat_axis=3, tiled=True)]
    gather x9 -> x0, local copies, waits for them, and re-layouts: 7.21 us -> none  [the longest x4 4.04 us: model_residual(): second_gain = jnp.take(gains, second_station, axis=3)[:, :, :, None, :]]
    mul x12 -> x0, other arithmetic: 6 us -> none  [the longest x3 5.96 us: normal_terms(): angular * pred_cross]
    add x22 -> x0, other arithmetic: 4.2 us -> none  [the longest x8 2.69 us: add_block(): return running_total + jnp.stack([real_part, imag_part], axis=1)]
  transfers between devices with their start and end apart: 2 -> 0, of which waited for: 2 -> 0; matrix products, arithmetic and copies ran while one was open for 2% -> 0% of each run, Pallas kernels for 0% -> 0%
where the time goes in v1:
time: 35.5 us; the launch traced here: 35.4 us
  Pallas kernels  32 us (90%)
  local copies, waits for them, and re-layouts  2.67 us (8%)
  between operations  0.65 us (2%)
    pallas_call x1, Pallas kernels, shards(): pl.pallas_call(functools.partial(kernel, sizes), out_shape=(jax.ShapeDtyp...  32 us
    unnamed x4, local copies, waits for them, and re-layouts  2.67 us

profile of v1, /device:TPU:0, one launch (start us, length us, event | category | flops | bytes accessed | tf_op | source)
XLA Modules:
  0.0 35.4 jit_solution(17680709812419806007)
XLA Ops:
  0.6 32.0 %shard_map.86 = (f32[2,2,1,384,128]{4,3,2,1,0:T(8,128)}, f32[3,2,1,512]{3,2,1,0:T(1,128)}) custom-call(f32[2,2,2,192,128]{4,3,2,1,0:T(8,128)} %vis.1, f32[2,2,128]{2,1,0:T(2,128)} %uv.1, f32[2,64]{1,0:T(2,128)} %lm.1, f32[2,64]{1,0:T(2,128)} %flux.1, s32[1,128]{1,0:T(1,128)} %bitcast.1, s32[2,128]{1,0:T(2,128)} %pairs.1, s32[2]{0:T(128)} %owner.1), custom_call_target="tpu_custom_call" | custom-call | tf_op jit(solution)/shard_map/pallas_call | solution.py:492
  32.7 0.0 copy-start
  32.7 2.1 %copy.11 = f32[2,2,1,384,128]{4,3,2,1,0:T(8,128)} copy(f32[2,2,1,384,128]{4,3,2,1,0:T(8,128)} %get-tuple-element.4) | data formatting | bytes 1572864
  34.8 0.0 copy-done
  34.8 0.6 %copy.12 = f32[3,2,1,512]{3,2,1,0:T(1,128)} copy(f32[3,2,1,512]{3,2,1,0:T(1,128)S(1)} %copy-done) | data formatting | bytes 24576
Async XLA Ops:
  32.7 2.1 %copy-start = (f32[3,2,1,512]{3,2,1,0:T(1,128)S(1)}, f32[3,2,1,512]{3,2,1,0:T(1,128)}, u32[]{:S(2)}) copy-start(f32[3,2,1,512]{3,2,1,0:T(1,128)} %get-tuple-element.5) | copy-start | bytes 36868

commit v2 on v1

--- a/solution.py
+++ b/solution.py
@@ -80,6 +80,7 @@
     onehot,
     terms,
     gathered,
+    trig,
     v_send,
     v_recv,
     p_send,
@@ -129,17 +130,23 @@
             for t in range(slots)
         ]
 
-    def averaged(rows, k, r):
-        total = rows[0] * vis[k, r, 0]
-        for t in range(1, slots):
-            total = total + rows[t] * vis[k, r, t]
-        return total
+    def average(rows, put):
+        def block(n, _):
+            k, r = n // 2, lax.rem(n, 2)
+            total = rows[0] * vis[k, r, 0]
+            for t in range(1, slots):
+                total = total + rows[t] * vis[k, r, t]
+            put(k, r, total)
+            return 0
+
+        lax.fori_loop(0, 4, block, 0)
 
     for step in range(1, ch_count):
-        rows = weight_rows(ch_peer(step))
-        for k in range(2):
-            for r in range(2):
-                sbuf[step - 1, k, r] = averaged(rows, k, r)
+
+        def put_away(k, r, value, step=step):
+            sbuf[step - 1, k, r] = value
+
+        average(weight_rows(ch_peer(step)), put_away)
     own_rows = weight_rows(ch)
     own_span = pl.ds(pl.multiple_of(ch * chan_local, 8), chan_local)
     for i in range(2):
@@ -173,9 +180,11 @@
         copy.start()
         p_copies.append(copy)
     pall[bl] = psend[...]
-    for k in range(2):
-        for r in range(2):
-            vbuf[k, r, own_span, :] = averaged(own_rows, k, r)
+
+    def put_own(k, r, value):
+        vbuf[k, r, own_span, :] = value
+
+    average(own_rows, put_own)
 
     def geo_row(s, _):
         for t in range(slots):
@@ -221,17 +230,23 @@
         lax.fori_loop(0, sources, centre, 0, unroll=4)
 
     zero = jnp.zeros((8, LANES), jnp.float32)
-    moments = [[zero, zero, zero] for _ in range(2)]
-    for first in range(0, half, TILE):
-        count = min(TILE, half - first)
-
-        def add_source(row, acc, first=first, count=count):
+
+    def channel_rows(d):
+        up = pl.ds(pl.multiple_of(8 * (half + d), 8), 8)
+        down = pl.ds(pl.multiple_of(8 * (half - 1 - d), 8), 8)
+        return up, down
+
+    def sky_tile(tile, moments):
+        first = tile * TILE
+        moments = list(moments)
+
+        def add_source(row, acc):
             span = pl.ds(pl.multiple_of(row * 8, 8), 8)
             fc = [ftab[k, 0, span, :] for k in range(2)]
             fs = [ftab[k, 1, span, :] for k in range(2)]
             out = []
             at = 0
-            for d in range(count):
+            for d in range(TILE):
                 cd = jnp.broadcast_to(dtab[first + d, 0, pl.ds(row, 1), :], (8, LANES))
                 sd = jnp.broadcast_to(dtab[first + d, 1, pl.ds(row, 1), :], (8, LANES))
                 for k in range(2):
@@ -242,13 +257,10 @@
                     at += 4
             return tuple(out)
 
-        acc = lax.fori_loop(
-            0, slots * sources, add_source, (zero,) * (8 * count), unroll=4
-        )
-        for d in range(count):
-            dist = jnp.float32(first + d + 0.5)
-            up = pl.ds(8 * (half + first + d), 8)
-            down = pl.ds(8 * (half - 1 - first - d), 8)
+        acc = lax.fori_loop(0, slots * sources, add_source, (zero,) * (8 * TILE), unroll=4)
+        for d in range(TILE):
+            dist = (first + d).astype(jnp.float32) + 0.5
+            up, down = channel_rows(first + d)
             for k in range(2):
                 cc, ss, sc, cs = acc[(d * 2 + k) * 4 : (d * 2 + k) * 4 + 4]
                 up_r, up_i, dn_r, dn_i = cc - ss, sc + cs, cc + ss, sc - cs
@@ -259,15 +271,18 @@
                 up_p = up_r * up_r + up_i * up_i
                 dn_p = dn_r * dn_r + dn_i * dn_i
                 both = up_p + dn_p
-                moments[k][0] = moments[k][0] + both
-                moments[k][1] = moments[k][1] + dist * (up_p - dn_p)
-                moments[k][2] = moments[k][2] + (dist * dist) * both
+                moments[3 * k] = moments[3 * k] + both
+                moments[3 * k + 1] = moments[3 * k + 1] + dist * (up_p - dn_p)
+                moments[3 * k + 2] = moments[3 * k + 2] + (dist * dist) * both
+        return tuple(moments)
+
+    moments = lax.fori_loop(0, half // TILE, sky_tile, (zero,) * 6)
 
     def fold(value):
         return jnp.sum(value, axis=0, keepdims=True)
 
     for k in range(2):
-        a0, a1, a2 = moments[k]
+        a0, a1, a2 = moments[3 * k : 3 * k + 3]
         mall[me, pl.ds(k, 1), :] = fold(a0)
         mall[me, pl.ds(2 + k, 1), :] = fold(omega_c * a0 + omega_step * a1)
         mall[me, pl.ds(4 + k, 1), :] = fold(
@@ -297,21 +312,24 @@
     for copy in p_copies:
         copy.wait()
     station = lax.broadcasted_iota(jnp.int32, (stations, LANES), 0)
-    for b in range(bl_count):
+
+    def hot_block(b, _):
         for i in range(2):
             hot = (station == pall[b, pl.ds(i, 1), :]).astype(jnp.float32)
-            onehot[:, pl.ds(i * base_all + b * LANES, LANES)] = hot.astype(jnp.bfloat16)
+            lanes = pl.ds(pl.multiple_of(i * base_all + b * LANES, LANES), LANES)
+            onehot[:, lanes] = hot.astype(jnp.bfloat16)
+        return 0
+
+    lax.fori_loop(0, bl_count, hot_block, 0)
 
     for copy in v_copies:
         copy.wait()
 
-    for d in range(half):
-        up = pl.ds(8 * (half + d), 8)
-        down = pl.ds(8 * (half - 1 - d), 8)
-        at = pl.ds(8 * d, 8)
+    def product_rows(d, _):
+        at = pl.ds(pl.multiple_of(8 * d, 8), 8)
         for k in range(2):
             halves = []
-            for span in (up, down):
+            for span in channel_rows(d):
                 m_r, m_i = model[k, 0, span, :], model[k, 1, span, :]
                 v_r, v_i = vbuf[k, 0, span, :], vbuf[k, 1, span, :]
                 halves.append((m_r * v_r + m_i * v_i, m_r * v_i - m_i * v_r))
@@ -320,6 +338,9 @@
             xtab[k, 1, at, :] = u_i + l_i
             xtab[k, 2, at, :] = u_r - l_r
             xtab[k, 3, at, :] = u_i - l_i
+        return 0
+
+    lax.fori_loop(0, half, product_rows, 0, unroll=2)
 
     own_first = pl.ds(pl.multiple_of(bl * LANES, LANES), LANES)
     own_second = pl.ds(pl.multiple_of(base_all + bl * LANES, LANES), LANES)
@@ -335,8 +356,14 @@
     def delay_tables(k):
         tau = own_gain(4) - gathered[pl.ds(4 + k, 1), own_second]
         sin_d, cos_d = sincos_turns(dist_col * (tau * jnp.float32(8.0 / chans)))
-        sin_c, cos_c = sincos_turns(freq_c * tau)
-        return sin_d, cos_d, sin_c, cos_c
+        trig[k, 0] = cos_d
+        trig[k, 1] = sin_d
+        return sincos_turns(freq_c * tau)
+
+    def offset_pair(k, d):
+        cd = jnp.broadcast_to(trig[k, 0, pl.ds(d, 1), :], (8, LANES))
+        sd = jnp.broadcast_to(trig[k, 1, pl.ds(d, 1), :], (8, LANES))
+        return cd, sd
 
     gains = (
         jnp.ones((2, stations), jnp.float32),
@@ -347,45 +374,45 @@
     gathered[pl.ds(2, 14), :] = jnp.zeros((14, 2 * base_all), jnp.float32)
     terms[pl.ds(12, 4), :] = jnp.zeros((4, 2 * base_all), jnp.float32)
 
-    for it in range(ITERS):
-        for k in range(2):
-            if it > 0:
-                sin_d, cos_d, sin_c, cos_c = delay_tables(k)
-            u_r, u_i, w_r, w_i = zero, zero, zero, zero
-            for d in range(half):
-                at = pl.ds(8 * d, 8)
+    for copy in m_copies:
+        copy.wait()
+
+    def newton_step(it, gains):
+        centres = [delay_tables(k) for k in range(2)]
+
+        def add_offset(d, acc):
+            at = pl.ds(pl.multiple_of(8 * d, 8), 8)
+            dist = d.astype(jnp.float32) + 0.5
+            out = []
+            for k in range(2):
+                u_r, u_i, w_r, w_i = acc[4 * k : 4 * k + 4]
                 p_r, p_i = xtab[k, 0, at, :], xtab[k, 1, at, :]
                 m_r, m_i = xtab[k, 2, at, :], xtab[k, 3, at, :]
-                dist = jnp.float32(d + 0.5)
-                if it > 0:
-                    cd, sd = cos_d[d : d + 1, :], sin_d[d : d + 1, :]
-                    u_r = u_r + (cd * p_r + sd * m_i)
-                    u_i = u_i + (cd * p_i - sd * m_r)
-                    cd, sd = dist * cd, dist * sd
-                    w_r = w_r + (cd * m_r + sd * p_i)
-                    w_i = w_i + (cd * m_i - sd * p_r)
-                else:
-                    u_r = u_r + p_r
-                    u_i = u_i + p_i
-                    w_r = w_r + dist * m_r
-                    w_i = w_i + dist * m_i
+                cd, sd = offset_pair(k, d)
+                u_r = u_r + (cd * p_r + sd * m_i)
+                u_i = u_i + (cd * p_i - sd * m_r)
+                cd, sd = dist * cd, dist * sd
+                w_r = w_r + (cd * m_r + sd * p_i)
+                w_i = w_i + (cd * m_i - sd * p_r)
+                out += [u_r, u_i, w_r, w_i]
+            return tuple(out)
+
+        acc = lax.fori_loop(0, half, add_offset, (zero,) * 8, unroll=4)
+        for k in range(2):
+            u_r, u_i, w_r, w_i = acc[4 * k : 4 * k + 4]
+            sin_c, cos_c = centres[k]
             w_r = omega_c * u_r + omega_step * w_r
             w_i = omega_c * u_i + omega_step * w_i
-            if it > 0:
-                u_r, u_i = cos_c * u_r + sin_c * u_i, cos_c * u_i - sin_c * u_r
-                w_r, w_i = cos_c * w_r + sin_c * w_i, cos_c * w_i - sin_c * w_r
+            u_r, u_i = cos_c * u_r + sin_c * u_i, cos_c * u_i - sin_c * u_r
+            w_r, w_i = cos_c * w_r + sin_c * w_i, cos_c * w_i - sin_c * w_r
             for n, value in enumerate((u_r, u_i, w_r, w_i)):
                 yall[it, me, pl.ds(2 * n + k, 1), :] = fold(value)
-        copies = spread(yall.at[it, me], y_send.at[it], y_recv.at[it])
-        if it == 0:
-            for copy in m_copies:
-                copy.wait()
-        for copy in copies:
+        for copy in spread(yall.at[it, me], y_send.at[it], y_recv.at[it]):
             copy.wait()
 
-        for b in range(bl_count):
-            lane_1 = pl.ds(b * LANES, LANES)
-            lane_2 = pl.ds(base_all + b * LANES, LANES)
+        def term_block(b, _):
+            lane_1 = pl.ds(pl.multiple_of(b * LANES, LANES), LANES)
+            lane_2 = pl.ds(pl.multiple_of(base_all + b * LANES, LANES), LANES)
             uj, wj = gathered[pl.ds(0, 2), lane_2], gathered[pl.ds(2, 2), lane_2]
             nj = uj * uj + wj * wj
             second = [jnp.zeros((2, LANES), jnp.float32)] * 6
@@ -421,6 +448,9 @@
                 second = [a + c for a, c in zip(second, more)]
             for x in range(6):
                 terms[pl.ds(2 * x, 2), lane_2] = second[x]
+            return 0
+
+        lax.fori_loop(0, bl_count, term_block, 0, unroll=2)
 
         summed = lax.dot_general(
             split3(terms[...]),
@@ -447,23 +477,26 @@
         )
         got = jnp.dot(split3(rows), onehot[...], preferred_element_type=jnp.float32)
         gathered[...] = got[0:16] + got[16:32] + got[32:48]
+        return gains
+
+    gains = lax.fori_loop(0, ITERS, newton_step, gains)
 
     for n in range(3):
         gains_out[n, :, 0, :] = gains[n]
 
     for k in range(2):
-        sin_d, cos_d, sin_c, cos_c = delay_tables(k)
+        sin_c, cos_c = delay_tables(k)
         ui, wi = own_gain(0), own_gain(2)
         uj, wj = gathered[pl.ds(k, 1), own_second], gathered[pl.ds(2 + k, 1), own_second]
         g_r = ui * uj + wi * wj
         g_i = wi * uj - ui * wj
         e_r = g_r * cos_c - g_i * sin_c
         e_i = g_r * sin_c + g_i * cos_c
-        for d in range(half):
-            cd, sd = cos_d[d : d + 1, :], sin_d[d : d + 1, :]
+
+        def residual_rows(d, _, k=k, e_r=e_r, e_i=e_i):
+            cd, sd = offset_pair(k, d)
             c_r, c_i, s_r, s_i = e_r * cd, e_i * cd, e_r * sd, e_i * sd
-            up = pl.ds(8 * (half + d), 8)
-            down = pl.ds(8 * (half - 1 - d), 8)
+            up, down = channel_rows(d)
             for span, f_r, f_i in (
                 (up, c_r - s_i, c_i + s_r),
                 (down, c_r + s_i, c_i - s_r),
@@ -471,6 +504,9 @@
                 m_r, m_i = model[k, 0, span, :], model[k, 1, span, :]
                 res_out[k, 0, 0, span, :] = vbuf[k, 0, span, :] - (f_r * m_r - f_i * m_i)
                 res_out[k, 1, 0, span, :] = vbuf[k, 1, span, :] - (f_r * m_i + f_i * m_r)
+            return 0
+
+        lax.fori_loop(0, half, residual_rows, 0, unroll=4)
 
 
 def shards(
@@ -512,6 +548,7 @@
             pltpu.VMEM((stations, 2 * bl_count * LANES), jnp.bfloat16),
             pltpu.VMEM((16, 2 * bl_count * LANES), f32),
             pltpu.VMEM((16, 2 * bl_count * LANES), f32),
+            pltpu.VMEM((2, 2, half, LANES), f32),
             dma((ch_count - 1,)),
             dma((ch_count - 1,)),
             dma((bl_count - 1,)),

time: 35.5 us -> 40 us (1.13)
  Pallas kernels: 32 us -> 36.5 us
    pallas_call x1, Pallas kernels: 32 us -> 36.5 us  [shards(): pl.pallas_call(functools.partial(kernel, sizes), out_shape=(jax.ShapeDtyp...]
where the time goes in v2:
time: 40 us; the launch traced here: 39.8 us
  Pallas kernels  36.5 us (91%)
  local copies, waits for them, and re-layouts  2.67 us (7%)
  between operations  0.65 us (2%)
    pallas_call x1, Pallas kernels, shards(): pl.pallas_call(functools.partial(kernel, sizes), out_shape=(jax.ShapeDtyp...  36.5 us
    unnamed x4, local copies, waits for them, and re-layouts  2.67 us

profile of v2, /device:TPU:0, one launch (start us, length us, event | category | flops | bytes accessed | tf_op | source)
XLA Modules:
  0.0 39.8 jit_solution(6410459209640805866)
XLA Ops:
  0.6 36.5 %shard_map.86 = (f32[2,2,1,384,128]{4,3,2,1,0:T(8,128)}, f32[3,2,1,512]{3,2,1,0:T(1,128)}) custom-call(f32[2,2,2,192,128]{4,3,2,1,0:T(8,128)} %vis.1, f32[2,2,128]{2,1,0:T(2,128)} %uv.1, f32[2,64]{1,0:T(2,128)} %lm.1, f32[2,64]{1,0:T(2,128)} %flux.1, s32[1,128]{1,0:T(1,128)} %bitcast.1, s32[2,128]{1,0:T(2,128)} %pairs.1, s32[2]{0:T(128)} %owner.1), custom_call_target="tpu_custom_call" | custom-call | tf_op jit(solution)/shard_map/pallas_call | solution.py:528
  37.1 0.0 copy-start
  37.1 2.1 %copy.11 = f32[2,2,1,384,128]{4,3,2,1,0:T(8,128)} copy(f32[2,2,1,384,128]{4,3,2,1,0:T(8,128)} %get-tuple-element.4) | data formatting | bytes 1572864
  39.2 0.0 copy-done
  39.2 0.6 %copy.12 = f32[3,2,1,512]{3,2,1,0:T(1,128)} copy(f32[3,2,1,512]{3,2,1,0:T(1,128)S(1)} %copy-done) | data formatting | bytes 24576
Async XLA Ops:
  37.1 2.1 %copy-start = (f32[3,2,1,512]{3,2,1,0:T(1,128)S(1)}, f32[3,2,1,512]{3,2,1,0:T(1,128)}, u32[]{:S(2)}) copy-start(f32[3,2,1,512]{3,2,1,0:T(1,128)} %get-tuple-element.5) | copy-start | bytes 36868

commit v3 on v1

--- a/solution.py
+++ b/solution.py
@@ -57,7 +57,7 @@
 
 def kernel(
     sizes,
-    vis,
+    vis_hbm,
     uv,
     lm,
     flux,
@@ -88,6 +88,8 @@
     m_recv,
     y_send,
     y_recv,
+    vis,
+    vis_sem,
 ):
     ch_count, bl_count, pol_count, slots, chan_local, chans, sources, stations = sizes
     ch = lax.axis_index("ch")
@@ -105,6 +107,8 @@
         other = lax.rem(me + step, group)
         return {"bl": other // pol_count, "pol": lax.rem(other, pol_count)}
 
+    load = pltpu.make_async_copy(vis_hbm, vis, vis_sem)
+    load.start()
     barrier = pltpu.get_barrier_semaphore()
     for step in range(1, ch_count):
         pl.semaphore_signal(
@@ -135,17 +139,61 @@
             total = total + rows[t] * vis[k, r, t]
         return total
 
+    own_rows = weight_rows(ch)
+    own_span = pl.ds(pl.multiple_of(ch * chan_local, 8), chan_local)
+    for i in range(2):
+        psend[pl.ds(i, 1), :] = pairs[pl.ds(i, 1), :]
+    psend[pl.ds(2, 6), :] = jnp.zeros((6, LANES), jnp.int32)
+
+    def geo_row(s, _):
+        for t in range(slots):
+            geo[pl.ds(t * sources + s, 1), :] = -(
+                lm[0, s] * uv[0, pl.ds(t, 1), :] + lm[1, s] * uv[1, pl.ds(t, 1), :]
+            )
+        return 0
+
+    lax.fori_loop(0, sources, geo_row, 0, unroll=8)
+
+    def offset_rows(block, _):
+        span = pl.ds(pl.multiple_of(block * 32, 32), 32)
+        sin_h, cos_h = sincos_turns(geo[span, :] * jnp.float32(4.0 / chans))
+        cos_f = cos_h * cos_h - sin_h * sin_h
+        sin_f = 2.0 * sin_h * cos_h
+        for d in range(half):
+            dtab[d, 0, span, :] = cos_h
+            dtab[d, 1, span, :] = sin_h
+            cos_h, sin_h = cos_h * cos_f - sin_h * sin_f, sin_h * cos_f + cos_h * sin_f
+        return 0
+
+    lax.fori_loop(0, slots * sources // 32, offset_rows, 0)
+
+    sub = lax.broadcasted_iota(jnp.int32, (8, LANES), 0).astype(jnp.float32)
+    freq_c = 0.5 + (sub + jnp.float32(4 * (chans // 8 - 1) + 0.5)) / chans
+    omega_c = two_pi * freq_c
+    omega_step = jnp.float32(two_pi * 8.0 / chans)
+
+    for t in range(slots):
+        wide = jnp.broadcast_to(own_rows[t], (8, LANES))
+
+        def centre(s, _, t=t, wide=wide):
+            row = t * sources + s
+            sin_c, cos_c = sincos_turns(geo[pl.ds(row, 1), :] * freq_c)
+            sin_c = sin_c * wide
+            cos_c = cos_c * wide
+            span = pl.ds(pl.multiple_of(row * 8, 8), 8)
+            for k in range(2):
+                ftab[k, 0, span, :] = flux[k, s] * cos_c
+                ftab[k, 1, span, :] = flux[k, s] * sin_c
+            return 0
+
+        lax.fori_loop(0, sources, centre, 0, unroll=4)
+
+    load.wait()
     for step in range(1, ch_count):
         rows = weight_rows(ch_peer(step))
         for k in range(2):
             for r in range(2):
                 sbuf[step - 1, k, r] = averaged(rows, k, r)
-    own_rows = weight_rows(ch)
-    own_span = pl.ds(pl.multiple_of(ch * chan_local, 8), chan_local)
-    for i in range(2):
-        psend[pl.ds(i, 1), :] = pairs[pl.ds(i, 1), :]
-    psend[pl.ds(2, 6), :] = jnp.zeros((6, LANES), jnp.int32)
-
     pl.semaphore_wait(barrier, ch_count - 1 + group - 1)
 
     v_copies = []
@@ -176,49 +224,6 @@
     for k in range(2):
         for r in range(2):
             vbuf[k, r, own_span, :] = averaged(own_rows, k, r)
-
-    def geo_row(s, _):
-        for t in range(slots):
-            geo[pl.ds(t * sources + s, 1), :] = -(
-                lm[0, s] * uv[0, pl.ds(t, 1), :] + lm[1, s] * uv[1, pl.ds(t, 1), :]
-            )
-        return 0
-
-    lax.fori_loop(0, sources, geo_row, 0, unroll=8)
-
-    def offset_rows(block, _):
-        span = pl.ds(pl.multiple_of(block * 32, 32), 32)
-        sin_h, cos_h = sincos_turns(geo[span, :] * jnp.float32(4.0 / chans))
-        cos_f = cos_h * cos_h - sin_h * sin_h
-        sin_f = 2.0 * sin_h * cos_h
-        for d in range(half):
-            dtab[d, 0, span, :] = cos_h
-            dtab[d, 1, span, :] = sin_h
-            cos_h, sin_h = cos_h * cos_f - sin_h * sin_f, sin_h * cos_f + cos_h * sin_f
-        return 0
-
-    lax.fori_loop(0, slots * sources // 32, offset_rows, 0)
-
-    sub = lax.broadcasted_iota(jnp.int32, (8, LANES), 0).astype(jnp.float32)
-    freq_c = 0.5 + (sub + jnp.float32(4 * (chans // 8 - 1) + 0.5)) / chans
-    omega_c = two_pi * freq_c
-    omega_step = jnp.float32(two_pi * 8.0 / chans)
-
-    for t in range(slots):
-        wide = jnp.broadcast_to(own_rows[t], (8, LANES))
-
-        def centre(s, _, t=t, wide=wide):
-            row = t * sources + s
-            sin_c, cos_c = sincos_turns(geo[pl.ds(row, 1), :] * freq_c)
-            sin_c = sin_c * wide
-            cos_c = cos_c * wide
-            span = pl.ds(pl.multiple_of(row * 8, 8), 8)
-            for k in range(2):
-                ftab[k, 0, span, :] = flux[k, s] * cos_c
-                ftab[k, 1, span, :] = flux[k, s] * sin_c
-            return 0
-
-        lax.fori_loop(0, sources, centre, 0, unroll=4)
 
     zero = jnp.zeros((8, LANES), jnp.float32)
     moments = [[zero, zero, zero] for _ in range(2)]
@@ -495,7 +500,7 @@
             jax.ShapeDtypeStruct((2, 2, 1, chans, LANES), f32),
             jax.ShapeDtypeStruct((3, 2, 1, stations), f32),
         ),
-        in_specs=[vmem, vmem, smem, smem, vmem, vmem, smem],
+        in_specs=[pl.BlockSpec(memory_space=pl.ANY), vmem, smem, smem, vmem, vmem, smem],
         out_specs=(vmem, vmem),
         scratch_shapes=[
             pltpu.VMEM((2, 2, chans, LANES), f32),
@@ -520,6 +525,8 @@
             dma((group - 1,)),
             dma((ITERS, group - 1)),
             dma((ITERS, group - 1)),
+            pltpu.VMEM(visibility.shape, f32),
+            dma,
         ],
         compiler_params=pltpu.CompilerParams(
             collective_id=0, has_side_effects=True, vmem_limit_bytes=56 * 1024 * 1024

time: 35.5 us -> 35.1 us (0.989)
  Pallas kernels: 32 us -> 31.6 us
    pallas_call x1, Pallas kernels: 32 us -> 31.6 us  [shards(): pl.pallas_call(functools.partial(kernel, sizes), out_shape=(jax.ShapeDtyp...]
where the time goes in v3:
time: 35.1 us; the launch traced here: 35 us
  Pallas kernels  31.6 us (90%)
  local copies, waits for them, and re-layouts  2.67 us (8%)
  between operations  0.65 us (2%)
    pallas_call x1, Pallas kernels, shards(): pl.pallas_call(functools.partial(kernel, sizes), out_shape=(jax.ShapeDtyp...  31.6 us
    unnamed x4, local copies, waits for them, and re-layouts  2.67 us

profile of v3, /device:TPU:0, one launch (start us, length us, event | category | flops | bytes accessed | tf_op | source)
XLA Modules:
  0.0 35.0 jit_solution(8815297090027794901)
XLA Ops:
  0.6 31.6 %shard_map.86 = (f32[2,2,1,384,128]{4,3,2,1,0:T(8,128)}, f32[3,2,1,512]{3,2,1,0:T(1,128)}) custom-call(f32[2,2,2,192,128]{4,3,2,1,0:T(8,128)} %vis_hbm.1, f32[2,2,128]{2,1,0:T(2,128)} %uv.1, f32[2,64]{1,0:T(2,128)} %lm.1, f32[2,64]{1,0:T(2,128)} %flux.1, s32[1,128]{1,0:T(1,128)} %bitcast.1, s32[2,128]{1,0:T(2,128)} %pairs.1, s32[2]{0:T(128)} %owner.1), custom_call_target="tpu_custom_call" | custom-call | tf_op jit(solution)/shard_map/pallas_call | solution.py:497
  32.3 0.0 copy-start
  32.3 2.1 %copy.11 = f32[2,2,1,384,128]{4,3,2,1,0:T(8,128)} copy(f32[2,2,1,384,128]{4,3,2,1,0:T(8,128)} %get-tuple-element.4) | data formatting | bytes 1572864
  34.4 0.0 copy-done
  34.4 0.6 %copy.12 = f32[3,2,1,512]{3,2,1,0:T(1,128)} copy(f32[3,2,1,512]{3,2,1,0:T(1,128)S(1)} %copy-done) | data formatting | bytes 24576
Async XLA Ops:
  32.3 2.1 %copy-start = (f32[3,2,1,512]{3,2,1,0:T(1,128)S(1)}, f32[3,2,1,512]{3,2,1,0:T(1,128)}, u32[]{:S(2)}) copy-start(f32[3,2,1,512]{3,2,1,0:T(1,128)} %get-tuple-element.5) | copy-start | bytes 36868

commit v4 on v3

--- a/solution.py
+++ b/solution.py
@@ -64,7 +64,10 @@
     factor,
     pairs,
     owner,
-    res_out,
+    data_out,
+    model_out,
+    trig_out,
+    turn_out,
     gains_out,
     vbuf,
     sbuf,
@@ -90,6 +93,7 @@
     y_recv,
     vis,
     vis_sem,
+    out_sem,
 ):
     ch_count, bl_count, pol_count, slots, chan_local, chans, sources, stations = sizes
     ch = lax.axis_index("ch")
@@ -309,6 +313,13 @@
 
     for copy in v_copies:
         copy.wait()
+
+    stores = [
+        pltpu.make_async_copy(vbuf, data_out, out_sem.at[0]),
+        pltpu.make_async_copy(model, model_out, out_sem.at[1]),
+    ]
+    for store in stores:
+        store.start()
 
     for d in range(half):
         up = pl.ds(8 * (half + d), 8)
@@ -462,20 +473,30 @@
         uj, wj = gathered[pl.ds(k, 1), own_second], gathered[pl.ds(2 + k, 1), own_second]
         g_r = ui * uj + wi * wj
         g_i = wi * uj - ui * wj
-        e_r = g_r * cos_c - g_i * sin_c
-        e_i = g_r * sin_c + g_i * cos_c
-        for d in range(half):
-            cd, sd = cos_d[d : d + 1, :], sin_d[d : d + 1, :]
-            c_r, c_i, s_r, s_i = e_r * cd, e_i * cd, e_r * sd, e_i * sd
-            up = pl.ds(8 * (half + d), 8)
-            down = pl.ds(8 * (half - 1 - d), 8)
-            for span, f_r, f_i in (
-                (up, c_r - s_i, c_i + s_r),
-                (down, c_r + s_i, c_i - s_r),
-            ):
-                m_r, m_i = model[k, 0, span, :], model[k, 1, span, :]
-                res_out[k, 0, 0, span, :] = vbuf[k, 0, span, :] - (f_r * m_r - f_i * m_i)
-                res_out[k, 1, 0, span, :] = vbuf[k, 1, span, :] - (f_r * m_i + f_i * m_r)
+        trig_out[k, 0] = cos_d
+        trig_out[k, 1] = sin_d
+        turn_out[k, 0] = g_r * cos_c - g_i * sin_c
+        turn_out[k, 1] = g_r * sin_c + g_i * cos_c
+    for store in stores:
+        store.wait()
+
+
+def residual_kernel(data, model, trig, turn, gains, res_out, gains_out):
+    gains_out[...] = gains[...]
+    half = trig.shape[2]
+    e_r, e_i = turn[0, 0], turn[0, 1]
+    for d in range(half):
+        cd, sd = trig[0, 0, pl.ds(d, 1), :], trig[0, 1, pl.ds(d, 1), :]
+        c_r, c_i, s_r, s_i = e_r * cd, e_i * cd, e_r * sd, e_i * sd
+        up = pl.ds(8 * (half + d), 8)
+        down = pl.ds(8 * (half - 1 - d), 8)
+        for span, f_r, f_i in (
+            (up, c_r - s_i, c_i + s_r),
+            (down, c_r + s_i, c_i - s_r),
+        ):
+            m_r, m_i = model[0, 0, span, :], model[0, 1, span, :]
+            res_out[0, 0, 0, span, :] = data[0, 0, span, :] - (f_r * m_r - f_i * m_i)
+            res_out[0, 1, 0, span, :] = data[0, 1, span, :] - (f_r * m_i + f_i * m_r)
 
 
 def shards(
@@ -494,14 +515,18 @@
     vmem = pl.BlockSpec(memory_space=pltpu.VMEM)
     smem = pl.BlockSpec(memory_space=pltpu.SMEM)
     dma = pltpu.SemaphoreType.DMA
-    return pl.pallas_call(
+    anywhere = pl.BlockSpec(memory_space=pl.ANY)
+    solved = pl.pallas_call(
         functools.partial(kernel, sizes),
         out_shape=(
-            jax.ShapeDtypeStruct((2, 2, 1, chans, LANES), f32),
+            jax.ShapeDtypeStruct((2, 2, chans, LANES), f32),
+            jax.ShapeDtypeStruct((2, 2, chans, LANES), f32),
+            jax.ShapeDtypeStruct((2, 2, half, LANES), f32),
+            jax.ShapeDtypeStruct((2, 2, 8, LANES), f32),
             jax.ShapeDtypeStruct((3, 2, 1, stations), f32),
         ),
         in_specs=[pl.BlockSpec(memory_space=pl.ANY), vmem, smem, smem, vmem, vmem, smem],
-        out_specs=(vmem, vmem),
+        out_specs=(anywhere, anywhere, vmem, vmem, vmem),
         scratch_shapes=[
             pltpu.VMEM((2, 2, chans, LANES), f32),
             pltpu.VMEM((ch_count - 1, 2, 2, chan_local, LANES), f32),
@@ -527,6 +552,7 @@
             dma((ITERS, group - 1)),
             pltpu.VMEM(visibility.shape, f32),
             dma,
+            dma((2,)),
         ],
         compiler_params=pltpu.CompilerParams(
             collective_id=0, has_side_effects=True, vmem_limit_bytes=56 * 1024 * 1024
@@ -540,6 +566,28 @@
         station_pairs,
         slot_owner,
     )
+    rows = pl.BlockSpec((1, 2, chans, LANES), lambda k: (k, 0, 0, 0))
+    gain_spec = pl.BlockSpec((3, 2, 1, stations), lambda k: (0, 0, 0, 0))
+    return pl.pallas_call(
+        residual_kernel,
+        grid=(2,),
+        out_shape=(
+            jax.ShapeDtypeStruct((2, 2, 1, chans, LANES), f32),
+            jax.ShapeDtypeStruct((3, 2, 1, stations), f32),
+        ),
+        in_specs=[
+            rows,
+            rows,
+            pl.BlockSpec((1, 2, half, LANES), lambda k: (k, 0, 0, 0)),
+            pl.BlockSpec((1, 2, 8, LANES), lambda k: (k, 0, 0, 0)),
+            gain_spec,
+        ],
+        out_specs=(
+            pl.BlockSpec((1, 2, 1, chans, LANES), lambda k: (k, 0, 0, 0, 0)),
+            gain_spec,
+        ),
+        compiler_params=pltpu.CompilerParams(vmem_limit_bytes=60 * 1024 * 1024),
+    )(*solved)
 
 
 def solution(mesh):

time: 35.1 us -> 34.3 us (0.977)
  local copies, waits for them, and re-layouts: 2.67 us -> 0 us
  Pallas kernels: 31.6 us -> 33.5 us
    unnamed x4 -> x0, local copies, waits for them, and re-layouts: 2.67 us -> none
    pallas_call x0 -> x1, Pallas kernels: none -> 2.26 us  [shards(): pl.pallas_call(residual_kernel, grid=(2,), out_shape=(jax.ShapeDtypeStruc...]
    pallas_call x1, Pallas kernels: 31.6 us -> 31.2 us  [shards(): pl.pallas_call(functools.partial(kernel, sizes), out_shape=(jax.ShapeDtyp...]
where the time goes in v4:
time: 34.3 us; the launch traced here: 34.1 us
  Pallas kernels  33.5 us (98%)
  between operations  0.64 us (2%)
    pallas_call x1, Pallas kernels, shards(): pl.pallas_call(functools.partial(kernel, sizes), out_shape=(jax.ShapeDtyp...  31.2 us
    pallas_call x1, Pallas kernels, shards(): pl.pallas_call(residual_kernel, grid=(2,), out_shape=(jax.ShapeDtypeStruc...  2.26 us

profile of v4, /device:TPU:0, one launch (start us, length us, event | category | flops | bytes accessed | tf_op | source)
XLA Modules:
  0.0 34.1 jit_solution(12929560745830710938)
XLA Ops:
  0.6 31.2 %shard_map.86 = (f32[2,2,384,128]{3,2,1,0:T(8,128)}, f32[2,2,384,128]{3,2,1,0:T(8,128)}, f32[2,2,24,128]{3,2,1,0:T(8,128)}, f32[2,2,8,128]{3,2,1,0:T(8,128)}, f32[3,2,1,512]{3,2,1,0:T(1,128)}) custom-call(f32[2,2,2,192,128]{4,3,2,1,0:T(8,128)} %vis_hbm.1, f32[2,2,128]{2,1,0:T(2,128)} %uv.1, f32[2,64]{1,0:T(2,128)} %lm.1, f32[2,64]{1,0:T(2,128)} %flux.1, ...), custom_call_target="tpu_custom_call" | custom-call | tf_op jit(solution)/shard_map/pallas_call | solution.py:519
  31.9 2.3 %shard_map.87 = (f32[2,2,1,384,128]{4,3,2,1,0:T(8,128)}, f32[3,2,1,512]{3,2,1,0:T(1,128)}) custom-call(f32[2,2,384,128]{3,2,1,0:T(8,128)} %get-tuple-element.7.data, f32[2,2,384,128]{3,2,1,0:T(8,128)} %get-tuple-element.8.model, f32[2,2,24,128]{3,2,1,0:T(8,128)} %get-tuple-element.9.trig, f32[2,2,8,128]{3,2,1,0:T(8,128)} %get-tuple-element.10.turn, ...), custom_call_target="tpu_custom_call" | custom-call | tf_op jit(solution)/shard_map/pallas_call | solution.py:571
